TPU v7x, 32 devices: a whole 2x2x4 slice. The times are simulated.
32 devices in a mesh: depth: 8 (over z, y), tile: 4 (over x, core).
Axes of the slice: x: 2, y: 2, z: 4, core: 2. Of those that a mesh axis runs over, the one named last changes fastest.
Arguments:
- ensemble: bfloat16 [64, 8, 64, 8192], P('tile', None, 'depth'), may hold values from -8 to 8
- active: int32 [8, 64], P('depth'), may hold values from 0 to 1, as said below
- depth_rank: int32 [8], replicated, may hold values from 0 to 7, as said below
Outputs:
- picture: float32 [4, 4, 65536], P(None, 'tile', 'depth')
Inputs may be any that keep to these rules, and one draw needn't show every extreme that they name: Every slab has exactly 32 active bricks. depth_rank[s] = s XOR k for one integer k.
All inputs are finite; a program needn't handle non-finite values.
Results may differ from a plain program's by a relative error of at most 0.0003.
Values may be sent and summed in bfloat16 or wider, within the bound.
A program may use at most 128 MiB of HBM per device.

v0:
```python
import jax
import jax.numpy as jnp
from jax import lax
from jax.sharding import PartitionSpec as P

BZ = 2
SHARPNESS = 4.0
ISOVALUE = 0.25
DENSITY = 0.35


def swapped(x, axis, apart):
    return lax.ppermute(x, axis, [(i, i ^ 1 << apart) for i in range(lax.axis_size(axis))])


def illuminate(mean_field, variance, above_prob):
    spread = jnp.sqrt(variance + 1e-06)
    depth_sum = jnp.cumsum(above_prob, axis=-2)
    transmit = jnp.exp(-DENSITY * (depth_sum - above_prob))
    weight = transmit * (1.0 - jnp.exp(-DENSITY * above_prob))
    red_sum = jnp.sum(weight * jax.nn.sigmoid(2.0 * mean_field), axis=-2)
    green_sum = jnp.sum(weight * (spread / (1.0 + spread)), axis=-2)
    blue_sum = jnp.sum(weight * above_prob, axis=-2)
    opacity = 1.0 - jnp.exp(-DENSITY * depth_sum[..., -1, :])
    return jnp.stack([red_sum, green_sum, blue_sum, opacity])


def render_members(samples):
    mean_field = jnp.mean(samples, axis=0)
    variance = jnp.mean((samples - mean_field) ** 2, axis=0)
    above_prob = jnp.mean(jax.nn.sigmoid(SHARPNESS * (samples - ISOVALUE)), axis=0)
    return illuminate(mean_field, variance, above_prob)


def body(ensemble, active, depth_rank):
    tile_count = lax.axis_size("tile")
    tile_id = lax.axis_index("tile")
    depth_count = lax.axis_size("depth")
    depth_id = lax.axis_index("depth")
    cells = ensemble.shape[3]
    brick_total = active.shape[1]
    per_tile = brick_total // tile_count
    pixels = cells // BZ
    flag_row = active[0]
    own_flags = lax.dynamic_slice_in_dim(flag_row, tile_id * per_tile, per_tile).astype(jnp.float32)
    regrouped = lax.all_to_all(
        lax.all_to_all(ensemble, "depth", split_axis=1, concat_axis=2, tiled=True),
        "tile",
        split_axis=2,
        concat_axis=0,
        tiled=True,
    )
    samples = regrouped.astype(jnp.float32).reshape(regrouped.shape[0], per_tile, BZ, pixels)
    shaded = render_members(samples) * own_flags[None, :, None]
    block_len = per_tile * pixels // depth_count
    image_rows = shaded.reshape(4, depth_count, block_len)
    own_rank = depth_rank[depth_id]
    current = image_rows
    for section in range(depth_count.bit_length() - 1):
        paired = current.reshape(4, current.shape[1] // 2, 2, block_len)
        my_bit = depth_id >> section & 1
        kept = jnp.where(my_bit == 1, paired[:, :, 1], paired[:, :, 0])
        handed = jnp.where(my_bit == 1, paired[:, :, 0], paired[:, :, 1])
        partner = swapped(handed, "depth", section)
        partner_rank = depth_rank[depth_id ^ 1 << section]
        mine_front = own_rank < partner_rank
        front_part = jnp.where(mine_front, kept, partner)
        back_part = jnp.where(mine_front, partner, kept)
        current = front_part + (1.0 - front_part[3:4]) * back_part
    return current


def solution(mesh):
    in_specs = (P("tile", None, "depth", None), P("depth", None), P())
    out_specs = P(None, "tile", "depth")
    return jax.shard_map(body, mesh=mesh, in_specs=in_specs, out_specs=out_specs, check_vma=False)
```

profile of v0, /device:TPU:0, one launch (start us, length us, event | category | flops | bytes accessed | tf_op | source)
XLA Modules:
  0.0 664.0 jit_solution(898726807793159516)
XLA Ops:
  0.0 8.5 %copy.45 = bf16[16,8,8,8192]{3,2,0,1:T(8,128)(2,1)S(1)} copy(bf16[16,8,8,8192]{3,2,1,0:T(8,128)(2,1)} %param.3) | data formatting | bytes 33554432 | tf_op args[0]
  8.5 369.9 %all_to_all.21 = bf16[16,8,8,8192]{3,2,0,1:T(8,128)(2,1)S(1)} all-to-all(bf16[16,8,8,8192]{3,2,0,1:T(8,128)(2,1)S(1)} %copy.45), channel_id=1, replica_groups=mesh['depth'=8,'tile'=4] {'depth'}, dimensions={1} | all-to-all | bytes 33554432 | tf_op jit(solution)/shard_map/all_to_all | solution.py:47
  378.4 2.2 copy.77
  380.6 25.1 %copy.47 = bf16[16,1,64,8192]{3,0,1,2:T(8,128)(2,1)} copy(bf16[16,1,64,8192]{3,2,0,1:T(8,128)(2,1)S(1)} %bitcast.87) | data formatting | bytes 33554432 | tf_op jit(solution)/shard_map/all_to_all | solution.py:47
  405.8 7.1 %all-to-all-start.1 = ((bf16[16,1,64,8192]{3,0,1,2:T(8,128)(2,1)}), bf16[16,1,64,8192]{3,0,1,2:T(8,128)(2,1)}, u32[]{:S(2)}, u32[]{:S(2)}) async-start(bf16[16,1,64,8192]{3,0,1,2:T(8,128)(2,1)} %copy.47), calls=%async_computation.1 | async-start | bytes 33554432 | tf_op jit(solution)/shard_map/all_to_all | solution.py:46
  413.5 182.4 %all-to-all-done.1 = bf16[16,1,64,8192]{3,0,1,2:T(8,128)(2,1)} async-done(((bf16[16,1,64,8192]{3,0,1,2:T(8,128)(2,1)}), bf16[16,1,64,8192]{3,0,1,2:T(8,128)(2,1)}, u32[]{:S(2)}, u32[]{:S(2)}) %all-to-all-start.1) | async-done | bytes 16777248 | tf_op jit(solution)/shard_map/all_to_all | solution.py:46
  595.9 7.0 %fusion.1 = f32[16,8192]{1,0:T(8,128)S(1)} fusion(bf16[16,1,4,16,8192]{4,0,3,2,1:T(8,128)(2,1)} %bitcast.6), kind=kLoop, calls=%fused_computation.2 | loop fusion | flops 16646144 | bytes 17301504 | tf_op jit(solution)/shard_map/reduce_sum | solution.py:29
  603.1 16.0 %fusion.9 = (f32[16,8192]{1,0:T(8,128)S(1)}, f32[16,8192]{1,0:T(8,128)S(1)}) fusion(bf16[16,1,4,16,8192]{4,0,3,2,1:T(8,128)(2,1)} %bitcast.6, f32[16,8192]{1,0:T(8,128)S(1)} %get-tuple-element.14), kind=kLoop, calls=%fused_computation.10 | loop fusion | flops 83623936 | bytes 18350080 | tf_op jit(solution)/shard_map/reduce_sum | solution.py:30
  621.1 2.7 reduce_window_sum.11
  623.9 1.0 fusion.16
  624.9 3.5 multiply_reduce_fusion.1
  628.3 1.1 stack.13
  629.4 1.1 stack.14
  631.5 1.0 fusion.21
  632.8 1.5 collective-permute-start
  634.3 0.7 fusion.22
  636.3 10.0 %collective-permute-done = f32[4,4,8192]{2,1,0:T(4,128)S(1)} collective-permute-done((f32[4,4,8192]{2,1,0:T(4,128)S(1)}, f32[4,4,8192]{2,1,0:T(4,128)S(1)}, u32[]{:S(2)}, u32[]{:S(2)}) %collective-permute-start) | collective-permute-done | bytes 524320 | tf_op jit(solution)/shard_map/ppermute | solution.py:13
  646.4 0.7 broadcast_select_fusion.1
  647.1 0.7 multiply_add_fusion
  648.2 1.2 collective-permute-start.1
  650.6 4.6 collective-permute-done.1
  655.6 1.1 collective-permute-start.2
  658.1 4.9 collective-permute-done.2
  663.2 0.8 copy.57
  (29 shorter events, 5.0 us)
Async XLA Ops:
  405.8 7.1 %copy-start.1 = (s32[1,64]{1,0:T(1,128)S(1)}, s32[1,64]{1,0:T(1,128)}, u32[]{:S(2)}) copy-start(s32[1,64]{1,0:T(1,128)} %param.4) | copy-start | bytes 772
  405.8 190.2 %all-to-all-start.1 = ((bf16[16,1,64,8192]{3,0,1,2:T(8,128)(2,1)}), bf16[16,1,64,8192]{3,0,1,2:T(8,128)(2,1)}, u32[]{:S(2)}, u32[]{:S(2)}) async-start(bf16[16,1,64,8192]{3,0,1,2:T(8,128)(2,1)} %copy.47), calls=%async_computation.1 | async-start | bytes 33554432 | tf_op jit(solution)/shard_map/all_to_all | solution.py:46
  603.1 31.3 %copy-start = (s32[8]{0:T(128)S(1)}, s32[8]{0:T(128)}, u32[]{:S(2)}) copy-start(s32[8]{0:T(128)} %param.5) | copy-start | bytes 100
  632.8 13.5 %collective-permute-start = (f32[4,4,8192]{2,1,0:T(4,128)S(1)}, f32[4,4,8192]{2,1,0:T(4,128)S(1)}, u32[]{:S(2)}, u32[]{:S(2)}) collective-permute-start(f32[4,4,8192]{2,1,0:T(4,128)S(1)} %bitcast.91), channel_id=1, source_target_pairs={{0,4},{4,0},{8,12},{12,8},{16,20},{20,16},{24,28},{28,24},{1,5},{5... | collective-permute-start | bytes 1572872 | tf_op jit(solution)/shard_map/ppermute | solution.py:13
  648.2 7.0 %collective-permute-start.1 = (f32[4,2,8192]{2,0,1:T(4,128)S(1)}, f32[4,2,8192]{2,0,1:T(4,128)S(1)}, u32[]{:S(2)}, u32[]{:S(2)}) collective-permute-start(f32[4,2,8192]{2,0,1:T(4,128)S(1)} %select_bitcast_fusion), channel_id=1, source_target_pairs={{0,8},{4,12},{8,0},{12,4},{16,24},{20,28},{24,16},{28,20},{1,9},{5... | collective-permute-start | bytes 786440 | tf_op jit(solution)/shard_map/ppermute | solution.py:13
  655.6 7.3 %collective-permute-start.2 = (f32[4,1,8192]{2,0,1:T(4,128)S(1)}, f32[4,1,8192]{2,0,1:T(4,128)S(1)}, u32[]{:S(2)}, u32[]{:S(2)}) collective-permute-start(f32[4,1,8192]{2,0,1:T(4,128)S(1)} %select_bitcast_fusion.1), channel_id=1, source_target_pairs={{0,16},{4,20},{8,24},{12,28},{16,0},{20,4},{24,8},{28,12},{1,17},{... | collective-permute-start | bytes 393224 | tf_op jit(solution)/shard_map/ppermute | solution.py:13
where the time goes:
time: 664 us
  blocking collectives  370 us (56%)
  waiting for transfers between devices  202 us (30%)
  local copies, waits for them, and re-layouts  42.9 us (6%)
  other arithmetic  34.2 us (5%)
  starting transfers between devices  10.9 us (2%)
    all_to_all x1, blocking collectives, body(): lax.all_to_all(ensemble, 'depth', split_axis=1, concat_axis=2, tiled=True)  370 us
    all_to_all x1, waiting for transfers between devices, body(): lax.all_to_all(lax.all_to_all(ensemble, 'depth', split_axis=1, concat_axi...  182 us
    all_to_all x2, local copies, waits for them, and re-layouts, body(): lax.all_to_all(ensemble, 'depth', split_axis=1, concat_axis=2, tiled=True)  27.3 us
    ppermute x3, waiting for transfers between devices, swapped(): lax.ppermute(x, axis, [(i, i ^ 1 << apart) for i in range(lax.axis_size(a...  19.5 us
    reduce_sum x1, other arithmetic, render_members(): variance = jnp.mean((samples - mean_field) ** 2, axis=0)  16 us
  transfers between devices with their start and end apart: 4, of which 4 were waited for; matrix products, arithmetic and copies ran while one was open for 0% of the time, Pallas kernels for 0%

commit v1 on v0

--- a/solution.py
+++ b/solution.py
@@ -7,6 +7,12 @@
 SHARPNESS = 4.0
 ISOVALUE = 0.25
 DENSITY = 0.35
+supply_heaps = lambda shard_in: jnp.concatenate(
+    lax.all_to_all(
+        jnp.stack(jnp.split(shard_in, lax.axis_size("tile"), axis=2), axis=0), "tile", 0, 0
+    ),
+    axis=0,
+)
 
 
 def swapped(x, axis, apart):
@@ -43,12 +49,8 @@
     pixels = cells // BZ
     flag_row = active[0]
     own_flags = lax.dynamic_slice_in_dim(flag_row, tile_id * per_tile, per_tile).astype(jnp.float32)
-    regrouped = lax.all_to_all(
-        lax.all_to_all(ensemble, "depth", split_axis=1, concat_axis=2, tiled=True),
-        "tile",
-        split_axis=2,
-        concat_axis=0,
-        tiled=True,
+    regrouped = supply_heaps(
+        lax.all_to_all(ensemble, "depth", split_axis=1, concat_axis=2, tiled=True)
     )
     samples = regrouped.astype(jnp.float32).reshape(regrouped.shape[0], per_tile, BZ, pixels)
     shaded = render_members(samples) * own_flags[None, :, None]

time: 664 us -> 657 us (0.989)
  local copies, waits for them, and re-layouts: 42.9 us -> 23.7 us
  other arithmetic: 34.2 us -> 45.5 us
    all_to_all x2 -> x1, local copies, waits for them, and re-layouts: 27.3 us -> 2.18 us  [body(): lax.all_to_all(ensemble, 'depth', split_axis=1, concat_axis=2, tiled=True)]
    another operation x0 -> x1, other arithmetic: none -> 13.8 us  [jnp.stack(jnp.split(shard_in, lax.axis_size('tile'), axis=2), axis=0)]
where the time goes in v1:
time: 657 us; the launch traced here: 656 us
  blocking collectives  370 us (56%)
  waiting for transfers between devices  202 us (31%)
  other arithmetic  45.5 us (7%)
  local copies, waits for them, and re-layouts  23.7 us (4%)
  starting transfers between devices  10.9 us (2%)
    all_to_all x1, blocking collectives, body(): lax.all_to_all(ensemble, 'depth', split_axis=1, concat_axis=2, tiled=True)  370 us
    all_to_all x1, waiting for transfers between devices, lax.all_to_all(jnp.stack(jnp.split(shard_in, lax.axis_size('tile'), axis=...  182 us
    ppermute x3, waiting for transfers between devices, swapped(): lax.ppermute(x, axis, [(i, i ^ 1 << apart) for i in range(lax.axis_size(a...  19.5 us
    another operation x1, other arithmetic, jnp.stack(jnp.split(shard_in, lax.axis_size('tile'), axis=2), axis=0)  13.8 us
    reduce_sum x1, other arithmetic, render_members(): variance = jnp.mean((samples - mean_field) ** 2, axis=0)  13.7 us
  transfers between devices with their start and end apart: 4, of which 4 were waited for; matrix products, arithmetic and copies ran while one was open for 0% of the time, Pallas kernels for 0%

profile of v1, /device:TPU:0, one launch (start us, length us, event | category | flops | bytes accessed | tf_op | source)
XLA Modules:
  0.0 656.0 jit_solution(14176643432243912178)
XLA Ops:
  0.0 8.5 %copy.48 = bf16[16,8,8,8192]{3,2,0,1:T(8,128)(2,1)S(1)} copy(bf16[16,8,8,8192]{3,2,1,0:T(8,128)(2,1)} %param.3) | data formatting | bytes 33554432 | tf_op args[0]
  8.5 369.9 %all_to_all.17 = bf16[16,8,8,8192]{3,2,0,1:T(8,128)(2,1)S(1)} all-to-all(bf16[16,8,8,8192]{3,2,0,1:T(8,128)(2,1)S(1)} %copy.48), channel_id=1, replica_groups=mesh['depth'=8,'tile'=4] {'depth'}, dimensions={1} | all-to-all | bytes 33554432 | tf_op jit(solution)/shard_map/all_to_all | solution.py:53
  378.4 2.2 copy.79
  380.6 5.9 slice_bitcast_fusion.3
  386.5 13.8 %pad_maximum_fusion = bf16[4,16,1,16,8192]{4,3,1,2,0:T(8,128)(2,1)} fusion(bf16[1,16,1,16,8192]{4,3,1,2,0:T(8,128)(2,1)} %get-tuple-element.11, bf16[1,16,1,16,8192]{4,3,1,2,0:T(8,128)(2,1)} %get-tuple-element.12, bf16[1,16,1,16,8192]{4,3,1,2,0:T(8,128)(2,1)} %get-tuple-element.13, bf16[1,16,1,16,8192]{4,3,1,2,0:T(8,128)(2,1)} %get-tuple-element.10), kind=kLoop, calls=%fused_computation.11 | loop fusion | flops 25165824 | bytes 33554432 | tf_op jit(solution)/shard_map/stack | solution.py:12
  400.3 7.1 %all-to-all-start.1 = ((bf16[4,16,1,16,8192]{4,3,1,2,0:T(8,128)(2,1)}), bf16[4,16,1,16,8192]{4,3,1,2,0:T(8,128)(2,1)}, u32[]{:S(2)}, u32[]{:S(2)}) async-start(bf16[4,16,1,16,8192]{4,3,1,2,0:T(8,128)(2,1)} %pad_maximum_fusion), calls=%async_computation.1 | async-start | bytes 33554432 | tf_op jit(solution)/shard_map/all_to_all | solution.py:11
  408.1 182.4 %all-to-all-done.1 = bf16[4,16,1,16,8192]{4,3,1,2,0:T(8,128)(2,1)} async-done(((bf16[4,16,1,16,8192]{4,3,1,2,0:T(8,128)(2,1)}), bf16[4,16,1,16,8192]{4,3,1,2,0:T(8,128)(2,1)}, u32[]{:S(2)}, u32[]{:S(2)}) %all-to-all-start.1) | async-done | bytes 16777248 | tf_op jit(solution)/shard_map/all_to_all | solution.py:11
  590.5 6.8 %convert_reduce_fusion = f32[16,8192]{1,0:T(8,128)S(1)} fusion(bf16[4,16,1,16,8192]{4,3,1,2,0:T(8,128)(2,1)} %all-to-all-done.1), kind=kLoop, calls=%fused_computation.1 | loop fusion | flops 16646144 | bytes 17301504 | tf_op jit(solution)/shard_map/reduce_sum | solution.py:35
  597.4 13.7 %fusion.6 = (f32[16,8192]{1,0:T(8,128)S(1)}, f32[16,8192]{1,0:T(8,128)S(1)}) fusion(bf16[4,16,1,16,8192]{4,3,1,2,0:T(8,128)(2,1)} %all-to-all-done.1, f32[16,8192]{1,0:T(8,128)S(1)} %get-tuple-element.18), kind=kLoop, calls=%fused_computation.9 | loop fusion | flops 83623936 | bytes 18350080 | tf_op jit(solution)/shard_map/reduce_sum | solution.py:36
  613.2 2.7 reduce_window_sum.11
  615.9 1.0 fusion.13
  616.9 3.5 multiply_reduce_fusion.1
  620.4 1.1 stack.33
  621.5 1.1 stack.34
  623.5 1.0 fusion.18
  624.9 1.5 collective-permute-start
  628.4 10.0 %collective-permute-done = f32[4,4,8192]{2,1,0:T(4,128)S(1)} collective-permute-done((f32[4,4,8192]{2,1,0:T(4,128)S(1)}, f32[4,4,8192]{2,1,0:T(4,128)S(1)}, u32[]{:S(2)}, u32[]{:S(2)}) %collective-permute-start) | collective-permute-done | bytes 524320 | tf_op jit(solution)/shard_map/ppermute | solution.py:19
  638.4 0.7 broadcast_select_fusion.1
  639.1 0.7 multiply_add_fusion
  640.3 1.2 collective-permute-start.1
  642.7 4.6 collective-permute-done.1
  647.7 1.1 collective-permute-start.2
  650.2 4.9 collective-permute-done.2
  655.2 0.8 copy.59
  (30 shorter events, 5.7 us)
Async XLA Ops:
  400.3 7.1 %copy-start.1 = (s32[1,64]{1,0:T(1,128)S(1)}, s32[1,64]{1,0:T(1,128)}, u32[]{:S(2)}) copy-start(s32[1,64]{1,0:T(1,128)} %param.4) | copy-start | bytes 772
  400.3 190.1 %all-to-all-start.1 = ((bf16[4,16,1,16,8192]{4,3,1,2,0:T(8,128)(2,1)}), bf16[4,16,1,16,8192]{4,3,1,2,0:T(8,128)(2,1)}, u32[]{:S(2)}, u32[]{:S(2)}) async-start(bf16[4,16,1,16,8192]{4,3,1,2,0:T(8,128)(2,1)} %pad_maximum_fusion), calls=%async_computation.1 | async-start | bytes 33554432 | tf_op jit(solution)/shard_map/all_to_all | solution.py:11
  597.4 29.0 %copy-start = (s32[8]{0:T(128)S(1)}, s32[8]{0:T(128)}, u32[]{:S(2)}) copy-start(s32[8]{0:T(128)} %param.5) | copy-start | bytes 100
  624.9 13.5 %collective-permute-start = (f32[4,4,8192]{2,1,0:T(4,128)S(1)}, f32[4,4,8192]{2,1,0:T(4,128)S(1)}, u32[]{:S(2)}, u32[]{:S(2)}) collective-permute-start(f32[4,4,8192]{2,1,0:T(4,128)S(1)} %bitcast.73), channel_id=1, source_target_pairs={{0,4},{4,0},{8,12},{12,8},{16,20},{20,16},{24,28},{28,24},{1,5},{5... | collective-permute-start | bytes 1572872 | tf_op jit(solution)/shard_map/ppermute | solution.py:19
  640.3 7.0 %collective-permute-start.1 = (f32[4,2,8192]{2,0,1:T(4,128)S(1)}, f32[4,2,8192]{2,0,1:T(4,128)S(1)}, u32[]{:S(2)}, u32[]{:S(2)}) collective-permute-start(f32[4,2,8192]{2,0,1:T(4,128)S(1)} %select_bitcast_fusion), channel_id=1, source_target_pairs={{0,8},{4,12},{8,0},{12,4},{16,24},{20,28},{24,16},{28,20},{1,9},{5... | collective-permute-start | bytes 786440 | tf_op jit(solution)/shard_map/ppermute | solution.py:19
  647.7 7.3 %collective-permute-start.2 = (f32[4,1,8192]{2,0,1:T(4,128)S(1)}, f32[4,1,8192]{2,0,1:T(4,128)S(1)}, u32[]{:S(2)}, u32[]{:S(2)}) collective-permute-start(f32[4,1,8192]{2,0,1:T(4,128)S(1)} %select_bitcast_fusion.1), channel_id=1, source_target_pairs={{0,16},{4,20},{8,24},{12,28},{16,0},{20,4},{24,8},{28,12},{1,17},{... | collective-permute-start | bytes 393224 | tf_op jit(solution)/shard_map/ppermute | solution.py:19
